TPU v7x, 32 devices: a whole 2x2x4 slice. The times are simulated.
32 devices in a mesh: groups: 2 (over y), blk: 8 (over z, x), sub: 2 (over core).
Axes of the slice: x: 2, y: 2, z: 4, core: 2. Of those that a mesh axis runs over, the one named last changes fastest.
Arguments:
- embeddings: bfloat16 [32, 1024, 384], P(('groups', 'blk', 'sub')), parts along dimension 0, may hold values from -0.3046875 to 0.3046875
- local_scales: bfloat16 [32, 1024], P(('groups', 'blk', 'sub')), parts along dimension 0, may hold values from 0.796875 to 2.5
- start: bfloat16 [32, 1024, 64], P(('groups', 'blk', 'sub')), parts along dimension 0, may hold values from -6 to 6
- pairs: int32 [64, 2], P('groups'), parts along dimension 0, may hold values from 0 to 15, as said below
Outputs:
- basis: float32 [32, 1024, 64], P(('groups', 'blk', 'sub')), parts along dimension 0
There are 2 independent parts, one for each index of `groups`. A program takes and returns all parts, laid end to end along the dimension named above; each array names one. Nothing has to cross between parts.
Inputs may be any that keep to these rules, and one draw needn't show every extreme that they name: Block b lies on device b. Every pair has row block <= column block, and the column block's device index exceeds the row block's by 0 to 4. Pairs may repeat and stand in any order. The pairs whose row block lies on one device number 0 to 4, and some device has exactly 4.
All inputs are finite; a program needn't handle non-finite values.
Results may differ from a plain program's by a relative error of at most 0.0036.
Values may be sent and summed in bfloat16 or wider, within the bound.
A program may use at most 64 MiB of HBM per device.

v0:
```python
import math

import jax
import jax.numpy as jnp
from jax import lax
from jax.sharding import PartitionSpec as P

REACH = 4


def passed_along(value, axis, steps):
    count = lax.axis_size(axis)
    first, last = (max(0, -steps), min(count, count - steps))
    return lax.ppermute(value, axis, [(source, source + steps) for source in range(first, last)])


def affinity(left, right, left_scale, right_scale):
    cross = jnp.einsum("ad,bd->ab", left, right, preferred_element_type=jnp.float32)
    left_f = left.astype(jnp.float32)
    right_f = right.astype(jnp.float32)
    left_sq = jnp.sum(left_f * left_f, -1)
    right_sq = jnp.sum(right_f * right_f, -1)
    dist = left_sq[:, None] + right_sq[None, :] - 2.0 * cross
    scale = left_scale.astype(jnp.float32)[:, None] * right_scale.astype(jnp.float32)[None, :]
    return jnp.exp(-dist / scale).astype(jnp.bfloat16)


def fetch_blocks(own_emb, own_scale, own_vec):
    got_emb = [own_emb]
    got_scale = [own_scale]
    got_vec = [own_vec]
    for distance in range(1, REACH + 1):
        moved = passed_along((own_emb, own_scale, own_vec), ("blk", "sub"), -distance)
        got_emb.append(moved[0])
        got_scale.append(moved[1])
        got_vec.append(moved[2])
    return (jnp.concatenate(got_emb, 0), jnp.concatenate(got_scale, 0), jnp.concatenate(got_vec, 0))


def fetch_vectors(own_vec):
    got_vec = [own_vec]
    for distance in range(1, REACH + 1):
        moved = passed_along(own_vec, ("blk", "sub"), -distance)
        got_vec.append(moved)
    return jnp.concatenate(got_vec, 0)


def return_sums(window, blk_dev):
    total = window[:blk_dev]
    for distance in range(1, REACH + 1):
        piece = window[distance * blk_dev : (distance + 1) * blk_dev]
        total = total + passed_along(piece, ("blk", "sub"), distance)
    return total


def orthonormal(values):
    flat = values.reshape(-1, values.shape[-1])
    partial_gram = jnp.dot(flat.T, flat, precision=lax.Precision.HIGHEST)
    gram_sum = lax.psum(partial_gram, ("blk", "sub"))
    lower = jnp.linalg.cholesky(gram_sum)
    solved = lax.linalg.triangular_solve(lower, flat, left_side=False, lower=True, transpose_a=True)
    return solved.reshape(values.shape)


def local(embeddings, local_scales, start, pairs):
    devices = lax.axis_size(("blk", "sub"))
    my_index = lax.axis_index(("blk", "sub"))
    blk_dev = embeddings.shape[0]
    block_rows = embeddings.shape[1]
    width_k = start.shape[2]
    capacity = 4 * blk_dev
    base = my_index * blk_dev
    row_all = pairs[:, 0]
    col_all = pairs[:, 1]
    mine = (row_all // blk_dev == my_index).astype(jnp.int32)
    rank = jnp.cumsum(mine) - 1
    picked = (
        (mine[None, :] == 1) & (rank[None, :] == jnp.arange(capacity, dtype=jnp.int32)[:, None])
    ).astype(jnp.int32)
    present = jnp.sum(picked, 1)
    row_loc = jnp.where(present > 0, jnp.sum(picked * row_all[None, :], 1) - base, 0)
    col_loc = jnp.where(present > 0, jnp.sum(picked * col_all[None, :], 1) - base, 0)
    weights = present.astype(jnp.float32)
    win_emb, win_scale, win_vec = fetch_blocks(embeddings, local_scales, start)
    window_len = win_emb.shape[0]

    def make_tile(left_idx, right_idx):
        left = lax.dynamic_index_in_dim(win_emb, left_idx, 0, keepdims=False)
        right = lax.dynamic_index_in_dim(win_emb, right_idx, 0, keepdims=False)
        left_s = lax.dynamic_index_in_dim(win_scale, left_idx, 0, keepdims=False)
        right_s = lax.dynamic_index_in_dim(win_scale, right_idx, 0, keepdims=False)
        return affinity(left, right, left_s, right_s)

    def tile_step(carry, item):
        return (carry, make_tile(item[0], item[1]))

    def apply_operator(vectors, stored):

        def step(total, item):
            left_idx, right_idx, weight, slot = item
            tile = lax.dynamic_index_in_dim(stored, slot, 0, keepdims=False)
            right_vec = lax.dynamic_index_in_dim(vectors, right_idx, 0, keepdims=False)
            left_vec = lax.dynamic_index_in_dim(vectors, left_idx, 0, keepdims=False)
            toward_row = jnp.dot(tile, right_vec, preferred_element_type=jnp.float32) * weight
            toward_col = (
                jnp.einsum("ab,ak->bk", tile, left_vec, preferred_element_type=jnp.float32) * weight
            )
            total = total.at[left_idx].add(toward_row)
            total = total.at[right_idx].add(toward_col)
            return (total, None)

        empty = jnp.zeros((window_len, block_rows, width_k), jnp.float32)
        slots = jnp.arange(capacity, dtype=jnp.int32)
        window = lax.scan(step, empty, (row_loc, col_loc, weights, slots))[0]
        return return_sums(window, blk_dev)

    stored = lax.scan(tile_step, 0, (row_loc, col_loc))[1]
    first = apply_operator(win_vec, stored)
    q_first = orthonormal(first).astype(jnp.bfloat16)
    win_q = fetch_vectors(q_first)
    second = apply_operator(win_q, stored)
    total_rows = devices * blk_dev * block_rows
    return math.sqrt(total_rows) * orthonormal(second)


def solution(mesh):
    in_specs = (
        P(("groups", "blk", "sub"), None, None),
        P(("groups", "blk", "sub"), None),
        P(("groups", "blk", "sub"), None, None),
        P("groups", None),
    )
    out_specs = P(("groups", "blk", "sub"), None, None)
    return jax.shard_map(local, mesh=mesh, in_specs=in_specs, out_specs=out_specs, check_vma=False)
```

profile of v0, /device:TPU:0, one launch (start us, length us, event | category | flops | bytes accessed | tf_op | source)
XLA Modules:
  0.0 475.8 jit_solution(11033140616253945967)
XLA Ops:
  0.0 1.4 collective-permute-start
  1.4 1.3 collective-permute-start.1
  2.7 1.3 collective-permute-start.4
  4.0 1.3 collective-permute-start.5
  5.3 1.3 collective-permute-start.6
  10.3 1.3 collective-permute-start.7
  11.6 20.6 %collective-permute-done.5 = bf16[1,1024]{1,0:T(2,128)(2,1)S(1)} collective-permute-done((bf16[1,1024]{1,0:T(2,128)(2,1)}, bf16[1,1024]{1,0:T(2,128)(2,1)S(1)}, u32[]{:S(2)}, u32[]{:S(2)}) %collective-permute-start.5) | collective-permute-done | bytes 2080 | tf_op jit(solution)/shard_map/ppermute | solution.py:14
  33.5 1.3 collective-permute-start.9
  34.8 2.1 constant_dynamic-update-slice_fusion.4
  40.3 7.4 %collective-permute-done.9 = bf16[1,1024,64]{2,1,0:T(8,128)(2,1)S(1)} collective-permute-done((bf16[1,1024,64]{2,1,0:T(8,128)(2,1)S(1)}, bf16[1,1024,64]{2,1,0:T(8,128)(2,1)S(1)}, u32[]{:S(2)}, u32[]{:S(2)}) %collective-permute-start.9) | collective-permute-done | bytes 131104 | tf_op jit(solution)/shard_map/ppermute | solution.py:14
  50.0 8.3 %collective-permute-done.10 = bf16[1,1024,64]{2,1,0:T(8,128)(2,1)} collective-permute-done((bf16[1,1024,64]{2,1,0:T(8,128)(2,1)S(1)}, bf16[1,1024,64]{2,1,0:T(8,128)(2,1)}, u32[]{:S(2)}, u32[]{:S(2)}) %collective-permute-start.10) | collective-permute-done | bytes 131104 | tf_op jit(solution)/shard_map/ppermute | solution.py:14
  60.7 33.1 %collective-permute-done.11 = bf16[1,1024,64]{2,1,0:T(8,128)(2,1)S(1)} collective-permute-done((bf16[1,1024,64]{2,1,0:T(8,128)(2,1)S(1)}, bf16[1,1024,64]{2,1,0:T(8,128)(2,1)S(1)}, u32[]{:S(2)}, u32[]{:S(2)}) %collective-permute-start.11) | collective-permute-done | bytes 131104 | tf_op jit(solution)/shard_map/ppermute | solution.py:14
  93.8 2.1 constant_dynamic-update-slice_fusion.3
  96.8 2.1 constant_dynamic-update-slice_fusion.1
  99.9 46.0 %while.34 = (s32[]{:T(128)}, bf16[4,1024,1024]{2,1,0:T(8,128)(2,1)}, s32[4]{0:T(128)S(1)}, bf16[5,1024,384]{2,1,0:T(8,128)(2,1)}, s32[4]{0:T(128)S(1)}, /*index=...) while((s32[]{:T(128)}, bf16[4,1024,1024]{2,1,0:T(8,128)(2,1)}, s32[4]{0:T(128)S(1)}, ...), condition=%wide.region_7.8_spmd, body=%wide.region_4.7_spmd.sunk | while | flops 815005696 | bytes 5280465 | solution.py:117
  105.0 1.8 multiply_reduce_fusion.3
  106.8 4.6 bitcast_dynamic-update-slice_fusion.2
  116.5 1.8 multiply_reduce_fusion.3
  118.3 4.6 bitcast_dynamic-update-slice_fusion.2
  127.9 1.8 multiply_reduce_fusion.3
  129.8 4.6 bitcast_dynamic-update-slice_fusion.2
  139.4 1.8 multiply_reduce_fusion.3
  141.3 4.6 bitcast_dynamic-update-slice_fusion.2
  146.0 63.2 %while.35 = (s32[]{:T(128)}, f32[5,1024,64]{1,2,0:T(8,128)S(1)}, s32[4]{0:T(128)S(1)}, s32[4]{0:T(128)S(1)}, bf16[4,1024,1024]{2,1,0:T(8,128)(2,1)}, /*index=5*/...) while((s32[]{:T(128)}, f32[5,1024,64]{1,2,0:T(8,128)S(1)}, ...), condition=%wide.region_11.12_spmd, body=%wide.region_8.11_spmd.sunk | while | flops 268828736 | bytes 5771581 | solution.py:114
  154.9 3.6 fusion.132
  158.5 3.4 fusion.133
  170.7 3.6 fusion.132
  174.2 3.4 fusion.133
  186.5 3.6 fusion.132
  190.0 3.4 fusion.133
  202.3 3.6 fusion.132
  205.8 3.4 fusion.133
  209.3 1.3 collective-permute-start.12
  210.6 1.3 collective-permute-start.13
  211.9 6.6 %collective-permute-start.14 = (f32[1,1024,64]{1,2,0:T(8,128)S(1)}, f32[1,1024,64]{1,2,0:T(8,128)S(1)}, u32[]{:S(2)}, u32[]{:S(2)}) collective-permute-start(f32[1,1024,64]{1,2,0:T(8,128)S(1)} %get-tuple-element.259), channel_id=1, source_target_pairs={{0,3},{1,4},{2,5},{3,6},{4,7},{5,8},{6,9},{7,10},{8,11},{9,12},{10... | collective-permute-start | bytes 786440 | tf_op jit(solution)/shard_map/ppermute | solution.py:14
  218.5 3.6 collective-permute-start.15
  222.7 5.2 %collective-permute-done.15 = f32[1,1024,64]{1,2,0:T(8,128)S(1)} collective-permute-done((f32[1,1024,64]{1,2,0:T(8,128)S(1)}, f32[1,1024,64]{1,2,0:T(8,128)S(1)}, u32[]{:S(2)}, u32[]{:S(2)}) %collective-permute-start.15) | collective-permute-done | bytes 262176 | tf_op jit(solution)/shard_map/ppermute | solution.py:14
  228.4 66.0 %psum.14 = f32[64,64]{0,1:T(8,128)S(1)} all-reduce(f32[64,64]{0,1:T(8,128)S(1)} %fusion.97), channel_id=1, replica_groups=mesh['groups'=2,'blk'=8,'sub'=2] {'blk','sub'}, use_global_device_ids=true, to_apply=%region_12.13 | all-reduce | flops 4096 | bytes 32768 | tf_op jit(solution)/shard_map/psum | solution.py:59
  294.5 5.8 %cholesky.44 = f32[64,64]{1,0:T(8,128)S(1)} custom-call(f32[64,64]{1,0:T(8,128)S(1)} %fusion.104), custom_call_target="Cholesky" | custom-call | tf_op jit(solution)/shard_map/jit(cholesky)/cholesky | solution.py:60
  301.7 4.9 %custom-call.6 = f32[1,64,64]{1,2,0:T(8,128)S(1)} custom-call(f32[1,64,64]{2,1,0:T(8,128)S(1)} %fusion.99), custom_call_target="InvertDiagBlocksLowerTriangular" | custom-call | tf_op jit(solution)/shard_map/triangular_solve/custom-call.0 | solution.py:61
  307.0 1.3 collective-permute-start.16
  308.3 1.3 collective-permute-start.17
  309.6 1.3 collective-permute-start.18
  312.2 4.2 collective-permute-done.17
  316.4 1.6 collective-permute-done.18
  318.0 2.7 collective-permute-done.19
  321.6 61.8 %while.36 = (s32[]{:T(128)}, f32[5,1024,64]{1,2,0:T(8,128)S(1)}, s32[4]{0:T(128)S(1)}, s32[4]{0:T(128)S(1)}, bf16[4,1024,1024]{2,1,0:T(8,128)(2,1)}, /*index=5*/...) while((s32[]{:T(128)}, f32[5,1024,64]{1,2,0:T(8,128)S(1)}, ...), condition=%wide.region_18.21_spmd, body=%wide.region_15.20_spmd.sunk | while | flops 268828736 | bytes 5771581 | solution.py:114
  330.2 3.5 fusion.138
  333.7 3.3 fusion.139
  345.6 3.5 fusion.138
  349.1 3.3 fusion.139
  361.1 3.5 fusion.138
  364.6 3.3 fusion.139
  376.5 3.5 fusion.138
  380.0 3.3 fusion.139
  383.4 2.5 collective-permute-start.20
  385.9 3.1 collective-permute-start.21
  389.0 3.9 collective-permute-start.22
  392.9 1.5 collective-permute-start.23
  395.7 3.0 collective-permute-done.22
  398.8 2.2 collective-permute-done.23
  401.4 61.1 %psum.15 = f32[64,64]{0,1:T(8,128)S(1)} all-reduce(f32[64,64]{0,1:T(8,128)S(1)} %fusion.94), channel_id=1, replica_groups=mesh['groups'=2,'blk'=8,'sub'=2] {'blk','sub'}, use_global_device_ids=true, to_apply=%region_19.22 | all-reduce | flops 4096 | bytes 32768 | tf_op jit(solution)/shard_map/psum | solution.py:59
  462.6 5.8 %cholesky.55 = f32[64,64]{1,0:T(8,128)S(1)} custom-call(f32[64,64]{1,0:T(8,128)S(1)} %fusion.102), custom_call_target="Cholesky" | custom-call | tf_op jit(solution)/shard_map/jit(cholesky)/cholesky | solution.py:60
  469.8 4.9 %custom-call.7 = f32[1,64,64]{1,2,0:T(8,128)S(1)} custom-call(f32[1,64,64]{2,1,0:T(8,128)S(1)} %fusion.100), custom_call_target="InvertDiagBlocksLowerTriangular" | custom-call | tf_op jit(solution)/shard_map/triangular_solve/custom-call.0 | solution.py:61
  (125 shorter events, 54.0 us)
Async XLA Ops:
  0.0 47.7 %copy-start = (bf16[1,1024,384]{2,1,0:T(8,128)(2,1)S(1)}, bf16[1,1024,384]{2,1,0:T(8,128)(2,1)}, u32[]{:S(2)}) copy-start(bf16[1,1024,384]{2,1,0:T(8,128)(2,1)} %param.21) | copy-start | bytes 2359300
  0.0 40.3 %copy-start.3 = (bf16[1,1024]{1,0:T(2,128)(2,1)S(1)}, bf16[1,1024]{1,0:T(2,128)(2,1)}, u32[]{:S(2)}) copy-start(bf16[1,1024]{1,0:T(2,128)(2,1)} %param.22) | copy-start | bytes 6148
  0.0 93.8 %collective-permute-start = (bf16[1,1024,384]{2,1,0:T(8,128)(2,1)}, bf16[1,1024,384]{2,1,0:T(8,128)(2,1)}, u32[]{:S(2)}, u32[]{:S(2)}) collective-permute-start(bf16[1,1024,384]{2,1,0:T(8,128)(2,1)} %param.21), channel_id=1, source_target_pairs={{1,0},{2,1},{3,2},{4,3},{5,4},{6,5},{7,6},{8,7},{9,8},{10,9},{11,1... | collective-permute-start | bytes 2359304 | tf_op jit(solution)/shard_map/ppermute | solution.py:14
  1.4 94.5 %collective-permute-start.1 = (bf16[1,1024,384]{2,1,0:T(8,128)(2,1)}, bf16[1,1024,384]{2,1,0:T(8,128)(2,1)S(1)}, u32[]{:S(2)}, u32[]{:S(2)}) collective-permute-start(bf16[1,1024,384]{2,1,0:T(8,128)(2,1)} %param.21), channel_id=1, source_target_pairs={{2,0},{3,1},{4,2},{5,3},{6,4},{7,5},{8,6},{9,7},{10,8},{11,9},{12,... | collective-permute-start | bytes 2359304 | tf_op jit(solution)/shard_map/ppermute | solution.py:14
  2.7 7.5 %collective-permute-start.4 = (bf16[1,1024]{1,0:T(2,128)(2,1)}, bf16[1,1024]{1,0:T(2,128)(2,1)S(1)}, u32[]{:S(2)}, u32[]{:S(2)}) collective-permute-start(bf16[1,1024]{1,0:T(2,128)(2,1)} %param.22), channel_id=1, source_target_pairs={{1,0},{2,1},{3,2},{4,3},{5,4},{6,5},{7,6},{8,7},{9,8},{10,9},{11,1... | collective-permute-start | bytes 6152 | tf_op jit(solution)/shard_map/ppermute | solution.py:14
  4.0 28.2 %collective-permute-start.5 = (bf16[1,1024]{1,0:T(2,128)(2,1)}, bf16[1,1024]{1,0:T(2,128)(2,1)S(1)}, u32[]{:S(2)}, u32[]{:S(2)}) collective-permute-start(bf16[1,1024]{1,0:T(2,128)(2,1)} %param.22), channel_id=1, source_target_pairs={{2,0},{3,1},{4,2},{5,3},{6,4},{7,5},{8,6},{9,7},{10,8},{11,9},{12,... | collective-permute-start | bytes 6152 | tf_op jit(solution)/shard_map/ppermute | solution.py:14
  5.3 28.1 %collective-permute-start.6 = (bf16[1,1024]{1,0:T(2,128)(2,1)}, bf16[1,1024]{1,0:T(2,128)(2,1)S(1)}, u32[]{:S(2)}, u32[]{:S(2)}) collective-permute-start(bf16[1,1024]{1,0:T(2,128)(2,1)} %param.22), channel_id=1, source_target_pairs={{3,0},{4,1},{5,2},{6,3},{7,4},{8,5},{9,6},{10,7},{11,8},{12,9},{13... | collective-permute-start | bytes 6152 | tf_op jit(solution)/shard_map/ppermute | solution.py:14
  10.3 26.7 %collective-permute-start.7 = (bf16[1,1024]{1,0:T(2,128)(2,1)}, bf16[1,1024]{1,0:T(2,128)(2,1)S(1)}, u32[]{:S(2)}, u32[]{:S(2)}) collective-permute-start(bf16[1,1024]{1,0:T(2,128)(2,1)} %param.22), channel_id=1, source_target_pairs={{4,0},{5,1},{6,2},{7,3},{8,4},{9,5},{10,6},{11,7},{12,8},{13,9},{1... | collective-permute-start | bytes 6152 | tf_op jit(solution)/shard_map/ppermute | solution.py:14
  32.2 6.0 %collective-permute-start.8 = (bf16[1,1024,64]{2,1,0:T(8,128)(2,1)S(1)}, bf16[1,1024,64]{2,1,0:T(8,128)(2,1)S(1)}, u32[]{:S(2)}, u32[]{:S(2)}) collective-permute-start(bf16[1,1024,64]{2,1,0:T(8,128)(2,1)S(1)} %copy.32), channel_id=1, source_target_pairs={{1,0},{2,1},{3,2},{4,3},{5,4},{6,5},{7,6},{8,7},{9,8},{10,9},{11,1... | collective-permute-start | bytes 393224 | tf_op jit(solution)/shard_map/ppermute | solution.py:14
  33.5 14.3 %collective-permute-start.9 = (bf16[1,1024,64]{2,1,0:T(8,128)(2,1)S(1)}, bf16[1,1024,64]{2,1,0:T(8,128)(2,1)S(1)}, u32[]{:S(2)}, u32[]{:S(2)}) collective-permute-start(bf16[1,1024,64]{2,1,0:T(8,128)(2,1)S(1)} %copy.32), channel_id=1, source_target_pairs={{2,0},{3,1},{4,2},{5,3},{6,4},{7,5},{8,6},{9,7},{10,8},{11,9},{12,... | collective-permute-start | bytes 393224 | tf_op jit(solution)/shard_map/ppermute | solution.py:14
  36.9 59.9 %collective-permute-start.2 = (bf16[1,1024,384]{2,1,0:T(8,128)(2,1)}, bf16[1,1024,384]{2,1,0:T(8,128)(2,1)}, u32[]{:S(2)}, u32[]{:S(2)}) collective-permute-start(bf16[1,1024,384]{2,1,0:T(8,128)(2,1)} %param.21), channel_id=1, source_target_pairs={{3,0},{4,1},{5,2},{6,3},{7,4},{8,5},{9,6},{10,7},{11,8},{12,9},{13... | collective-permute-start | bytes 2359304 | tf_op jit(solution)/shard_map/ppermute | solution.py:14
  38.2 0.7 copy-start.1
  38.9 19.4 %collective-permute-start.10 = (bf16[1,1024,64]{2,1,0:T(8,128)(2,1)S(1)}, bf16[1,1024,64]{2,1,0:T(8,128)(2,1)}, u32[]{:S(2)}, u32[]{:S(2)}) collective-permute-start(bf16[1,1024,64]{2,1,0:T(8,128)(2,1)S(1)} %copy.32), channel_id=1, source_target_pairs={{3,0},{4,1},{5,2},{6,3},{7,4},{8,5},{9,6},{10,7},{11,8},{12,9},{13... | collective-permute-start | bytes 393224 | tf_op jit(solution)/shard_map/ppermute | solution.py:14
  47.8 51.2 %collective-permute-start.3 = (bf16[1,1024,384]{2,1,0:T(8,128)(2,1)S(1)}, bf16[1,1024,384]{2,1,0:T(8,128)(2,1)S(1)}, u32[]{:S(2)}, u32[]{:S(2)}) collective-permute-start(bf16[1,1024,384]{2,1,0:T(8,128)(2,1)S(1)} %copy-done), channel_id=1, source_target_pairs={{4,0},{5,1},{6,2},{7,3},{8,4},{9,5},{10,6},{11,7},{12,8},{13,9},{1... | collective-permute-start | bytes 2359304 | tf_op jit(solution)/shard_map/ppermute | solution.py:14
  58.3 35.4 %collective-permute-start.11 = (bf16[1,1024,64]{2,1,0:T(8,128)(2,1)S(1)}, bf16[1,1024,64]{2,1,0:T(8,128)(2,1)S(1)}, u32[]{:S(2)}, u32[]{:S(2)}) collective-permute-start(bf16[1,1024,64]{2,1,0:T(8,128)(2,1)S(1)} %copy.32), channel_id=1, source_target_pairs={{4,0},{5,1},{6,2},{7,3},{8,4},{9,5},{10,6},{11,7},{12,8},{13,9},{1... | collective-permute-start | bytes 393224 | tf_op jit(solution)/shard_map/ppermute | solution.py:14
  99.9 46.1 %copy-start.2 = (s32[3]{0:T(128)S(1)}, s32[3]{0:T(128)}, u32[]{:S(2)}) copy-start(s32[3]{0:T(128)} %constant.189.clone.1) | copy-start | bytes 40
  209.3 12.8 %collective-permute-start.12 = (f32[1,1024,64]{1,2,0:T(8,128)S(1)}, f32[1,1024,64]{1,2,0:T(8,128)S(1)}, u32[]{:S(2)}, u32[]{:S(2)}) collective-permute-start(f32[1,1024,64]{1,2,0:T(8,128)S(1)} %get-tuple-element.257), channel_id=1, source_target_pairs={{0,1},{1,2},{2,3},{3,4},{4,5},{5,6},{6,7},{7,8},{8,9},{9,10},{10,1... | collective-permute-start | bytes 786440 | tf_op jit(solution)/shard_map/ppermute | solution.py:14
  210.6 11.5 %collective-permute-start.13 = (f32[1,1024,64]{1,2,0:T(8,128)S(1)}, f32[1,1024,64]{1,2,0:T(8,128)S(1)}, u32[]{:S(2)}, u32[]{:S(2)}) collective-permute-start(f32[1,1024,64]{1,2,0:T(8,128)S(1)} %get-tuple-element.260), channel_id=1, source_target_pairs={{0,2},{1,3},{2,4},{3,5},{4,6},{5,7},{6,8},{7,9},{8,10},{9,11},{10,... | collective-permute-start | bytes 786440 | tf_op jit(solution)/shard_map/ppermute | solution.py:14
  211.9 10.8 %collective-permute-start.14 = (f32[1,1024,64]{1,2,0:T(8,128)S(1)}, f32[1,1024,64]{1,2,0:T(8,128)S(1)}, u32[]{:S(2)}, u32[]{:S(2)}) collective-permute-start(f32[1,1024,64]{1,2,0:T(8,128)S(1)} %get-tuple-element.259), channel_id=1, source_target_pairs={{0,3},{1,4},{2,5},{3,6},{4,7},{5,8},{6,9},{7,10},{8,11},{9,12},{10... | collective-permute-start | bytes 786440 | tf_op jit(solution)/shard_map/ppermute | solution.py:14
  218.5 9.4 %collective-permute-start.15 = (f32[1,1024,64]{1,2,0:T(8,128)S(1)}, f32[1,1024,64]{1,2,0:T(8,128)S(1)}, u32[]{:S(2)}, u32[]{:S(2)}) collective-permute-start(f32[1,1024,64]{1,2,0:T(8,128)S(1)} %get-tuple-element.258), channel_id=1, source_target_pairs={{0,4},{1,5},{2,6},{3,7},{4,8},{5,9},{6,10},{7,11},{8,12},{9,13},{1... | collective-permute-start | bytes 786440 | tf_op jit(solution)/shard_map/ppermute | solution.py:14
  307.0 5.2 %collective-permute-start.16 = (bf16[1,1024,64]{1,2,0:T(8,128)(2,1)S(1)}, bf16[1,1024,64]{1,2,0:T(8,128)(2,1)S(1)}, u32[]{:S(2)}, u32[]{:S(2)}) collective-permute-start(bf16[1,1024,64]{1,2,0:T(8,128)(2,1)S(1)} %get-tuple-element.267), channel_id=1, source_target_pairs={{1,0},{2,1},{3,2},{4,3},{5,4},{6,5},{7,6},{8,7},{9,8},{10,9},{11,1... | collective-permute-start | bytes 393224 | tf_op jit(solution)/shard_map/ppermute | solution.py:14
  308.3 8.1 %collective-permute-start.17 = (bf16[1,1024,64]{1,2,0:T(8,128)(2,1)S(1)}, bf16[1,1024,64]{1,2,0:T(8,128)(2,1)S(1)}, u32[]{:S(2)}, u32[]{:S(2)}) collective-permute-start(bf16[1,1024,64]{1,2,0:T(8,128)(2,1)S(1)} %get-tuple-element.267), channel_id=1, source_target_pairs={{2,0},{3,1},{4,2},{5,3},{6,4},{7,5},{8,6},{9,7},{10,8},{11,9},{12,... | collective-permute-start | bytes 393224 | tf_op jit(solution)/shard_map/ppermute | solution.py:14
  309.6 8.4 %collective-permute-start.18 = (bf16[1,1024,64]{1,2,0:T(8,128)(2,1)S(1)}, bf16[1,1024,64]{1,2,0:T(8,128)(2,1)S(1)}, u32[]{:S(2)}, u32[]{:S(2)}) collective-permute-start(bf16[1,1024,64]{1,2,0:T(8,128)(2,1)S(1)} %get-tuple-element.267), channel_id=1, source_target_pairs={{3,0},{4,1},{5,2},{6,3},{7,4},{8,5},{9,6},{10,7},{11,8},{12,9},{13... | collective-permute-start | bytes 393224 | tf_op jit(solution)/shard_map/ppermute | solution.py:14
  310.9 9.8 %collective-permute-start.19 = (bf16[1,1024,64]{1,2,0:T(8,128)(2,1)S(1)}, bf16[1,1024,64]{1,2,0:T(8,128)(2,1)S(1)}, u32[]{:S(2)}, u32[]{:S(2)}) collective-permute-start(bf16[1,1024,64]{1,2,0:T(8,128)(2,1)S(1)} %get-tuple-element.267), channel_id=1, source_target_pairs={{4,0},{5,1},{6,2},{7,3},{8,4},{9,5},{10,6},{11,7},{12,8},{13,9},{1... | collective-permute-start | bytes 393224 | tf_op jit(solution)/shard_map/ppermute | solution.py:14
  383.4 11.0 %collective-permute-start.20 = (f32[1,1024,64]{1,2,0:T(8,128)S(1)}, f32[1,1024,64]{1,2,0:T(8,128)S(1)}, u32[]{:S(2)}, u32[]{:S(2)}) collective-permute-start(f32[1,1024,64]{1,2,0:T(8,128)S(1)} %get-tuple-element.253), channel_id=1, source_target_pairs={{0,1},{1,2},{2,3},{3,4},{4,5},{5,6},{6,7},{7,8},{8,9},{9,10},{10,1... | collective-permute-start | bytes 786440 | tf_op jit(solution)/shard_map/ppermute | solution.py:14
  385.9 9.8 %collective-permute-start.21 = (f32[1,1024,64]{1,2,0:T(8,128)S(1)}, f32[1,1024,64]{1,2,0:T(8,128)S(1)}, u32[]{:S(2)}, u32[]{:S(2)}) collective-permute-start(f32[1,1024,64]{1,2,0:T(8,128)S(1)} %get-tuple-element.256), channel_id=1, source_target_pairs={{0,2},{1,3},{2,4},{3,5},{4,6},{5,7},{6,8},{7,9},{8,10},{9,11},{10,... | collective-permute-start | bytes 786440 | tf_op jit(solution)/shard_map/ppermute | solution.py:14
  389.0 9.8 %collective-permute-start.22 = (f32[1,1024,64]{1,2,0:T(8,128)S(1)}, f32[1,1024,64]{1,2,0:T(8,128)S(1)}, u32[]{:S(2)}, u32[]{:S(2)}) collective-permute-start(f32[1,1024,64]{1,2,0:T(8,128)S(1)} %get-tuple-element.255), channel_id=1, source_target_pairs={{0,3},{1,4},{2,5},{3,6},{4,7},{5,8},{6,9},{7,10},{8,11},{9,12},{10... | collective-permute-start | bytes 786440 | tf_op jit(solution)/shard_map/ppermute | solution.py:14
  392.9 8.0 %collective-permute-start.23 = (f32[1,1024,64]{1,2,0:T(8,128)S(1)}, f32[1,1024,64]{1,2,0:T(8,128)S(1)}, u32[]{:S(2)}, u32[]{:S(2)}) collective-permute-start(f32[1,1024,64]{1,2,0:T(8,128)S(1)} %get-tuple-element.254), channel_id=1, source_target_pairs={{0,4},{1,5},{2,6},{3,7},{4,8},{5,9},{6,10},{7,11},{8,12},{9,13},{1... | collective-permute-start | bytes 786440 | tf_op jit(solution)/shard_map/ppermute | solution.py:14
where the time goes:
time: 479 us; the launch traced here: 476 us
  blocking collectives  127 us (27%)
  waiting for transfers between devices  90.1 us (19%)
  matrix products  75.7 us (16%)
  loops' own time  60.7 us (13%)
  starting transfers between devices  44.5 us (9%)
  other arithmetic  39.1 us (8%)
  local copies, waits for them, and re-layouts  38.1 us (8%)
    psum x2, blocking collectives, orthonormal(): gram_sum = lax.psum(partial_gram, ('blk', 'sub'))  127 us
    ppermute x24, waiting for transfers between devices, passed_along(): lax.ppermute(value, axis, [(source, source + steps) for source in range(f...  90.1 us
    another operation x2, loops' own time, apply_operator(): window = lax.scan(step, empty, (row_loc, col_loc, weights, slots))[0]  45.1 us
    ppermute x24, starting transfers between devices, passed_along(): lax.ppermute(value, axis, [(source, source + steps) for source in range(f...  44.5 us
    dot_general x8, matrix products, step(): jnp.dot(tile, right_vec, preferred_element_type=jnp.float32) * weight  28.3 us
    dot_general x8, matrix products, step(): jnp.einsum('ab,ak->bk', tile, left_vec, preferred_element_type=jnp.float32)  26.7 us
    dynamic_slice x32, local copies, waits for them, and re-layouts, local(): stored = lax.scan(tile_step, 0, (row_loc, col_loc))[1]  18.9 us
    dot_general x4, matrix products, affinity(): jnp.einsum('ad,bd->ab', left, right, preferred_element_type=jnp.float32)  18.4 us
  transfers between devices with their start and end apart: 24, of which 12 were waited for; matrix products, arithmetic and copies ran while one was open for 3% of the time, Pallas kernels for 0%

commit v1 on v0

v1 whole, which is shorter than its diff:
```python
import functools
import math

import jax
import jax.numpy as jnp
from jax import lax
from jax.experimental import pallas as pl
from jax.experimental.pallas import tpu as pltpu
from jax.sharding import PartitionSpec as P

REACH = 4
CHUNKS = 4
STEP = 4
MESH = pl.DeviceIdType.MESH
HIGH = lax.Precision.HIGHEST
F32 = jnp.float32
BF16 = jnp.bfloat16
NN = (((1,), (0,)), ((), ()))
NT = (((1,), (1,)), ((), ()))


def inverse_factor(gram):
    size = gram.shape[0]
    eye = (
        lax.broadcasted_iota(jnp.int32, (size, size), 0)
        == lax.broadcasted_iota(jnp.int32, (size, size), 1)
    ).astype(F32)
    both = jnp.concatenate([gram, eye], 1)
    groups = [both[8 * g : 8 * g + 8] for g in range(size // 8)]
    below = lax.broadcasted_iota(jnp.int32, (8, 1), 0)
    done = []
    for j in range(0, size, STEP):
        g, r = divmod(j, 8)
        last = size // 8
        line = [groups[g][r + t : r + t + 1] for t in range(STEP)]
        head = [[line[t][:, j + u : j + u + 1] for u in range(STEP)] for t in range(STEP)]
        cols = [[groups[h][:, j + t : j + t + 1] for h in range(g, last)] for t in range(STEP)]
        inv = []
        for t in range(STEP):
            inv.append(1.0 / head[t][t])
            for u in range(t + 1, STEP):
                f = head[t][u] * inv[t]
                line[u] = line[u] - f * line[t]
                cols[u] = [cu - f * ct for cu, ct in zip(cols[u], cols[t])]
                head[u] = [hu - f * ht for hu, ht in zip(head[u], head[t])]
            done.append(line[t] * lax.rsqrt(head[t][t]))
        scaled = [line[t] * inv[t] for t in range(STEP)]
        for h in range(g, last):
            if h == g and r + STEP == 8:
                continue
            update = cols[0][h - g] * scaled[0]
            for t in range(1, STEP):
                update = update + cols[t][h - g] * scaled[t]
            if h == g:
                update = jnp.where(below >= r + STEP, update, 0.0)
            groups[h] = groups[h] - update
    return jnp.concatenate(done, 0)[:, size:]


def kernel(
    n, rows, width, k, stages, out_scale,
    pairs, scales, start_vec, emb, out,
    pack, col_aux,
    gemb, gpack, qown, gq, tiles, acc, part, got, gram, rowaux,
    mate, msend, mrecv, esend, erecv, qsend, qrecv, psend, precv, gsend, grecv,
):
    i = lax.axis_index(("blk", "sub"))
    core = lax.rem(i, 2)
    quad = lax.rem(i, 4)
    cw = rows // CHUNKS

    def to(dev):
        return {"blk": lax.div(dev, 2), "sub": lax.rem(dev, 2)}

    def remote(src, dst, ss, rs, dev):
        return pltpu.make_async_remote_copy(
            src_ref=src, dst_ref=dst, send_sem=ss, recv_sem=rs, device_id=to(dev), device_id_type=MESH
        )

    barrier = pltpu.get_barrier_semaphore()

    @pl.loop(1, n)
    def _(t):
        pl.semaphore_signal(barrier, inc=1, device_id=to(lax.rem(i + t, n)), device_id_type=MESH)

    pl.semaphore_wait(barrier, n - 1)

    def piece(slot, q):
        if q == 0:
            return pack if slot is None else gpack.at[slot]
        sl = pl.ds((q - 1) * cw, cw)
        return emb.at[sl] if slot is None else gemb.at[slot, sl]

    def send(kind, q, source, slot, dev):
        return remote(piece(source, q), piece(slot, q), esend.at[kind, q], erecv.at[slot, q], dev)

    def wait_piece(slot, q):
        remote(piece(slot, q), piece(slot, q), esend.at[0, q], erecv.at[slot, q], i).wait_recv()

    first_quad, later = quad < 2, quad >= 2
    one, zero = core == 1, core == 0
    own_sends = [
        (0, None, 3, i - 4, i >= 4),
        (1, None, 1, i - 2, later),
        (2, None, 0, i - 1, one),
    ]
    fwd4 = [
        (3, 3, 1, i + 2, first_quad & (i + 4 < n)),
        (5, 3, 2, i + 1, zero & (i + 4 < n)),
    ]
    fwd2 = [
        (4, 1, 2, i - 1, one & (i + 2 < n)),
        (6, 1, 0, i + 1, zero & (i + 2 < n)),
    ]

    def start(entries, q):
        for kind, source, slot, dev, cond in entries:
            @pl.when(cond)
            def _():
                send(kind, q, source, slot, dev).start()

    for q in range(1, CHUNKS + 1):
        start(own_sends, q)
        if q > 1:
            continue
        ones = jnp.ones((8, width), BF16)
        squares = []
        for c in range(CHUNKS):
            x = emb[c * cw : (c + 1) * cw, :].astype(F32)
            x = x * x
            big = x.astype(BF16)
            small = (x - big.astype(F32)).astype(BF16)
            squares.append(
                lax.dot_general(ones, big, NT, preferred_element_type=F32)
                + lax.dot_general(ones, small, NT, preferred_element_type=F32)
            )
        sq = jnp.concatenate(squares, 1)
        scale = scales[...].astype(F32)
        high = sq.astype(BF16).astype(F32)
        mid = (sq - high).astype(BF16).astype(F32)
        low = (sq - high) - mid
        line = lax.broadcasted_iota(jnp.int32, (8, rows), 0)
        tail = jnp.where(line == 0, high, jnp.where(line == 1, mid, jnp.where(line == 2, low, scale)))
        pack[k : k + 16, :] = jnp.concatenate([tail, tail], 0).astype(BF16)
        pack[0:k, :] = start_vec[...].astype(F32).T.astype(BF16)
        col_aux[...] = jnp.where(line == 0, 0.5 * sq, (2.0 / math.log(2.0)) / scale).T
        start(own_sends, 0)

    offset = pairs[:, 1:2] - i
    held = pairs[:, 0:1] == i
    m_ref = [
        jnp.sum((held & (offset == d)).astype(F32), 0, keepdims=True) for d in range(REACH + 1)
    ]

    def prepare_aux(slot):
        tail = (pack if slot is None else gpack.at[slot])[k : k + 16, :].astype(F32)
        idx = 0 if slot is None else slot + 1
        half = 0.5 * ((tail[0:1] + tail[1:2]) + tail[2:3])
        rowaux[idx, 0:1, :] = half
        rowaux[idx, 1:2, :] = 1.0 / tail[3:4]

    def make(d, q):
        cols = pl.ds(q * cw, cw)
        right = emb[cols, :] if d == 0 else gemb[d - 1, cols, :]
        half_r = rowaux[d, 0:1, cols]
        inv_r = rowaux[d, 1:2, cols]
        for r in range(4):
            rs = pl.ds(r * (rows // 4), rows // 4)
            cross = lax.dot_general(emb[rs, :], right, NT, preferred_element_type=F32)
            t = (cross - (col_aux[rs, 0:1] + half_r)) * (col_aux[rs, 1:2] * inv_r)
            tiles[d, rs, cols] = jnp.exp2(t).astype(BF16)

    def row_product(vec, d, q):
        cols = pl.ds(q * cw, cw)
        return lax.dot_general(vec[:, cols], tiles[d, :, cols], NT, preferred_element_type=F32)

    def part_copy(p, d, q):
        cols = pl.ds(q * cw, cw)
        return remote(
            part.at[p, d - 1, :, cols], got.at[p, d - 1, :, cols],
            psend.at[p, d - 1, q], precv.at[p, d - 1, q], lax.rem(i + d, n),
        )

    def mate_copy(slot, d, q):
        cols = pl.ds(q * cw, cw)
        return remote(
            part.at[1, d - 1, :, cols], mate.at[slot, :, cols],
            msend.at[slot, q], mrecv.at[slot, q], i + 1 - 2 * core,
        )

    def col_product(p, d, q, own_vec):
        cols = pl.ds(q * cw, cw)
        part[p, d - 1, :, cols] = m_ref[d] * lax.dot_general(
            own_vec, tiles[d, :, cols], NN, preferred_element_type=F32
        )
        if p == 0:
            part_copy(p, d, q).start()

    own_v = pack.at[pl.ds(0, k)]
    prepare_aux(None)
    acc[...] = jnp.zeros_like(acc)
    for q in range(CHUNKS):
        make(0, q)
        acc[...] += (2.0 * m_ref[0]) * row_product(own_v, 0, q)

    def arrive(d, q, then):
        @pl.when(i + d < n)
        def _():
            wait_piece(d - 1, q)
            if q == 0:
                prepare_aux(d - 1)
        start(then, q)

    for d, then in ((4, fwd4), (2, fwd2), (3, []), (1, [])):
        arrive(d, 0, then)

    for q in range(CHUNKS):
        arrive(4, q + 1, fwd4)
        arrive(2, q + 1, fwd2)
        for d in (4, 2, 3, 1):
            if d in (3, 1):
                arrive(d, q + 1, [])

            @pl.when(i + d < n)
            def _():
                make(d, q)
                col_product(0, d, q, own_v[...])
                acc[...] += m_ref[d] * row_product(gpack.at[d - 1, pl.ds(0, k)], d, q)

    def arrives(p, d):
        if p == 0 or d in (2, 4):
            return i - d >= 0
        return one if d == 1 else i < 0

    def finish_sum(p):
        for d in (1, 2, 3, 4):
            @pl.when(arrives(p, d))
            def _():
                for q in range(CHUNKS):
                    part_copy(p, d, q).wait_recv()
                acc[...] += got[p, d - 1]

    def factor(p):
        y = acc[...]
        total = lax.dot_general(y, y, NT, precision=HIGH, preferred_element_type=F32)
        total = jnp.concatenate([total[: k // 2], total[k // 2 :]], 1)
        for s, (stride, radix) in enumerate(stages):
            pos = lax.rem(lax.div(i, stride), radix)
            base = i - pos * stride
            gram[p, s, pos] = total
            copies = []
            for t in range(1, radix):
                peer = lax.rem(pos + t, radix)
                copies.append((
                    remote(gram.at[p, s, pos], gram.at[p, s, pos], gsend.at[p, s, t], grecv.at[p, s, pos], base + peer * stride),
                    remote(gram.at[p, s, pos], gram.at[p, s, peer], gsend.at[p, s, t], grecv.at[p, s, peer], base + peer * stride),
                ))
            for c, _ in copies:
                c.start()
            for c, w in copies:
                w.wait_recv()
            total = gram[p, s, 0]
            for t in range(1, radix):
                total = total + gram[p, s, t]
            for c, _ in copies:
                c.wait_send()
        total = jnp.concatenate([total[:, :k], total[:, k:]], 0)
        return lax.dot_general(inverse_factor(total), acc[...], NN, precision=HIGH, preferred_element_type=F32)

    finish_sum(0)
    qown[...] = factor(0).astype(BF16)

    def q_copy(d, dev):
        return remote(qown, gq.at[d - 1], qsend.at[d - 1], qrecv.at[d - 1], dev)

    for d in (4, 3, 2, 1):
        @pl.when(i - d >= 0)
        def _():
            q_copy(d, i - d).start()

    mates = [
        (0, 3, zero & (i + 3 < n)),
        (1, 3, one & (i + 3 < n)),
        (0, 1, one & (i + 1 < n)),
    ]
    for d in (3, 1, 2, 4):
        @pl.when(i + d < n)
        def _():
            for q in range(CHUNKS):
                col_product(1, d, q, qown[...])
        for slot, dist, cond in mates:
            if dist == d:
                @pl.when(cond)
                def _():
                    for q in range(CHUNKS):
                        mate_copy(slot, d, q).start()
        if d == 1:
            @pl.when(zero)
            def _():
                for q in range(CHUNKS):
                    part_copy(1, 1, q).start()
    for d in (4, 2):
        for q in range(CHUNKS):
            cols = pl.ds(q * cw, cw)
            if d == 4:
                @pl.when(zero & (i + 4 < n))
                def _():
                    mate_copy(1, 3, q).wait_recv()
                    part[1, 3, :, cols] += mate[1, :, cols]
            else:
                @pl.when(i + 2 < n)
                def _():
                    mate_copy(0, 1, q).wait_recv()
                    part[1, 1, :, cols] += mate[0, :, cols]

            @pl.when(i + d < n)
            def _():
                part_copy(1, d, q).start()

    acc[...] = jnp.zeros_like(acc)
    for q in range(CHUNKS):
        acc[...] += (2.0 * m_ref[0]) * row_product(qown, 0, q)
    for d in (1, 2, 3, 4):
        @pl.when(i + d < n)
        def _():
            q_copy(d, i).wait_recv()
            for q in range(CHUNKS):
                acc[...] += m_ref[d] * row_product(gq.at[d - 1], d, q)

    finish_sum(1)
    out[...] = out_scale * factor(1)

    for entries in (own_sends, fwd4, fwd2):
        for kind, source, slot, dev, cond in entries:
            @pl.when(cond)
            def _():
                for q in range(CHUNKS + 1):
                    send(kind, q, source, slot, dev).wait_send()
    for d in (1, 2, 3, 4):
        @pl.when(i - d >= 0)
        def _():
            q_copy(d, i).wait_send()

        for p in range(2):
            if p == 0 or d in (2, 4):
                sent = i + d < n
            elif d == 1:
                sent = zero
            else:
                continue

            @pl.when(sent)
            def _():
                for q in range(CHUNKS):
                    part_copy(p, d, q).wait_send()
    for slot, dist, cond in mates:
        @pl.when(cond)
        def _():
            for q in range(CHUNKS):
                mate_copy(slot, dist, q).wait_send()


def local(embeddings, local_scales, start, pairs):
    n = lax.axis_size("blk") * lax.axis_size("sub")
    i = lax.axis_index(("blk", "sub"))
    rows, width = embeddings.shape[1:]
    k = start.shape[2]
    stages = []
    stride = 1
    while stride < n:
        radix = min(4, n // stride)
        stages.append((stride, radix))
        stride *= radix
    ns = len(stages)
    vm = pl.BlockSpec(memory_space=pltpu.VMEM)
    dma = pltpu.SemaphoreType.DMA
    res = pl.pallas_call(
        functools.partial(kernel, n, rows, width, k, tuple(stages), math.sqrt(n * rows)),
        out_shape=jax.ShapeDtypeStruct((k, rows), F32),
        in_specs=[vm, vm, vm, vm],
        out_specs=vm,
        scratch_shapes=[
            pltpu.VMEM((k + 16, rows), BF16),
            pltpu.VMEM((rows, 8), F32),
            pltpu.VMEM((4, rows, width), BF16),
            pltpu.VMEM((4, k + 16, rows), BF16),
            pltpu.VMEM((k, rows), BF16),
            pltpu.VMEM((4, k, rows), BF16),
            pltpu.VMEM((5, rows, rows), BF16),
            pltpu.VMEM((k, rows), F32),
            pltpu.VMEM((2, 4, k, rows), F32),
            pltpu.VMEM((2, 4, k, rows), F32),
            pltpu.VMEM((2, ns, 4, k // 2, 2 * k), F32),
            pltpu.VMEM((5, 8, rows), F32),
            pltpu.VMEM((2, k, rows), F32),
            dma((2, CHUNKS)),
            dma((2, CHUNKS)),
            dma((7, CHUNKS + 1)),
            dma((4, CHUNKS + 1)),
            dma((4,)),
            dma((4,)),
            dma((2, 4, CHUNKS)),
            dma((2, 4, CHUNKS)),
            dma((2, ns, 4)),
            dma((2, ns, 4)),
        ],
        compiler_params=pltpu.CompilerParams(
            collective_id=0, has_side_effects=True, vmem_limit_bytes=56 * 1024 * 1024
        ),
    )(pairs, local_scales, start[0], embeddings[0])
    return res.T[None]


def solution(mesh):
    in_specs = (
        P(("groups", "blk", "sub"), None, None),
        P(("groups", "blk", "sub"), None),
        P(("groups", "blk", "sub"), None, None),
        P("groups", None),
    )
    out_specs = P(("groups", "blk", "sub"), None, None)
    return jax.shard_map(local, mesh=mesh, in_specs=in_specs, out_specs=out_specs, check_vma=False)
```

time: 479 us -> 102 us (0.21)
  blocking collectives: 127 us -> 0 us
  Pallas kernels: 0 us -> 97.4 us
  waiting for transfers between devices: 90.1 us -> 0 us
  matrix products: 75.7 us -> 0 us
  loops' own time: 60.7 us -> 0 us
  starting transfers between devices: 44.5 us -> 0 us
  other arithmetic: 39.1 us -> 0 us
  local copies, waits for them, and re-layouts: 38.1 us -> 4.77 us
    psum x2 -> x0, blocking collectives: 127 us -> none  [orthonormal(): gram_sum = lax.psum(partial_gram, ('blk', 'sub'))]
    pallas_call x0 -> x1, Pallas kernels: none -> 97.4 us  [local(): pl.pallas_call(functools.partial(kernel, n, rows, width, k, tuple(stages)...]
    ppermute x24 -> x0, waiting for transfers between devices: 90.1 us -> none  [passed_along(): lax.ppermute(value, axis, [(source, source + steps) for source in range(f...]
    dot_general x22 -> x0, matrix products: 74.1 us -> none  [the longest x8 28.3 us: step(): jnp.dot(tile, right_vec, preferred_element_type=jnp.float32) * weight]
    another operation x3 -> x0, loops' own time: 60.7 us -> none  [the longest x2 45.1 us: apply_operator(): window = lax.scan(step, empty, (row_loc, col_loc, weights, slots))[0]]
    ppermute x24 -> x0, starting transfers between devices: 44.5 us -> none  [passed_along(): lax.ppermute(value, axis, [(source, source + steps) for source in range(f...]
    another operation x19 -> x0, other arithmetic: 30 us -> none  [the longest x6 13 us: orthonormal(): lower = jnp.linalg.cholesky(gram_sum)]
    dynamic_slice x40 -> x0, local copies, waits for them, and re-layouts: 23.7 us -> none  [the longest x32 18.9 us: local(): stored = lax.scan(tile_step, 0, (row_loc, col_loc))[1]]
  transfers between devices with their start and end apart: 24 -> 0, of which waited for: 12 -> 0; matrix products, arithmetic and copies ran while one was open for 3% -> 0% of each run, Pallas kernels for 0% -> 0%
where the time goes in v1:
time: 102 us
  Pallas kernels  97.4 us (95%)
  local copies, waits for them, and re-layouts  4.77 us (5%)
    pallas_call x1, Pallas kernels, local(): pl.pallas_call(functools.partial(kernel, n, rows, width, k, tuple(stages)...  97.4 us
    unnamed x5, local copies, waits for them, and re-layouts  4.77 us

profile of v1, /device:TPU:0, one launch (start us, length us, event | category | flops | bytes accessed | tf_op | source)
XLA Modules:
  0.0 102.2 jit_solution(4579655671102699352)
XLA Ops:
  0.0 0.0 copy-start
  0.0 0.7 copy-done
  0.7 0.7 copy.6.pairs
  1.4 1.7 %copy.5 = bf16[1,1024,64]{2,1,0:T(8,128)(2,1)} copy(bf16[1,1024,64]{1,2,0:T(8,128)(2,1)} %param.6) | data formatting | bytes 262144 | tf_op args[2]
  3.1 97.4 %shard_map.46 = f32[64,1024]{1,0:T(8,128)} custom-call(s32[32,2]{1,0:T(8,128)} %copy.6.pairs, bf16[1,1024]{1,0:T(2,128)(2,1)} %scales.1, bf16[1024,64]{1,0:T(8,128)(2,1)} %bitcast.6, bf16[1024,384]{1,0:T(8,128)(2,1)} %bitcast.7), custom_call_target="tpu_custom_call" | custom-call | tf_op jit(solution)/shard_map/pallas_call | solution.py:377
  100.5 1.7 %copy.8 = f32[1,1024,64]{1,2,0:T(8,128)} copy(f32[1,1024,64]{1,2,0:T(8,128)} %bitcast.5) | data formatting | bytes 524288
Async XLA Ops:
  0.0 0.7 copy-start

commit v2 on v1

--- a/solution.py
+++ b/solution.py
@@ -10,7 +10,7 @@
 
 REACH = 4
 CHUNKS = 4
-STEP = 4
+STEP = 2
 MESH = pl.DeviceIdType.MESH
 HIGH = lax.Precision.HIGHEST
 F32 = jnp.float32
@@ -214,18 +214,27 @@
     for d, then in ((4, fwd4), (2, fwd2), (3, []), (1, [])):
         arrive(d, 0, then)
 
-    for q in range(CHUNKS):
-        arrive(4, q + 1, fwd4)
-        arrive(2, q + 1, fwd2)
-        for d in (4, 2, 3, 1):
-            if d in (3, 1):
-                arrive(d, q + 1, [])
-
-            @pl.when(i + d < n)
-            def _():
-                make(d, q)
-                col_product(0, d, q, own_v[...])
-                acc[...] += m_ref[d] * row_product(gpack.at[d - 1, pl.ds(0, k)], d, q)
+    def work(d, q):
+        @pl.when(i + d < n)
+        def _():
+            make(d, q)
+            col_product(0, d, q, own_v[...])
+            acc[...] += m_ref[d] * row_product(gpack.at[d - 1, pl.ds(0, k)], d, q)
+
+    for q in range(CHUNKS + 1):
+        if q < CHUNKS:
+            arrive(4, q + 1, fwd4)
+        if q > 0:
+            arrive(3, q, [])
+            work(3, q - 1)
+        if q < CHUNKS:
+            arrive(2, q + 1, fwd2)
+        if q > 0:
+            arrive(1, q, [])
+            work(1, q - 1)
+        if q < CHUNKS:
+            work(4, q)
+            work(2, q)
 
     def arrives(p, d):
         if p == 0 or d in (2, 4):
@@ -286,8 +295,9 @@
     for d in (3, 1, 2, 4):
         @pl.when(i + d < n)
         def _():
-            for q in range(CHUNKS):
-                col_product(1, d, q, qown[...])
+            part[1, d - 1] = m_ref[d] * lax.dot_general(
+                qown[...], tiles[d], NN, preferred_element_type=F32
+            )
         for slot, dist, cond in mates:
             if dist == d:
                 @pl.when(cond)
@@ -317,15 +327,16 @@
             def _():
                 part_copy(1, d, q).start()
 
-    acc[...] = jnp.zeros_like(acc)
-    for q in range(CHUNKS):
-        acc[...] += (2.0 * m_ref[0]) * row_product(qown, 0, q)
+    acc[...] = (2.0 * m_ref[0]) * lax.dot_general(
+        qown[...], tiles[0], NT, preferred_element_type=F32
+    )
     for d in (1, 2, 3, 4):
         @pl.when(i + d < n)
         def _():
             q_copy(d, i).wait_recv()
-            for q in range(CHUNKS):
-                acc[...] += m_ref[d] * row_product(gq.at[d - 1], d, q)
+            acc[...] += m_ref[d] * lax.dot_general(
+                gq[d - 1], tiles[d], NT, preferred_element_type=F32
+            )
 
     finish_sum(1)
     out[...] = out_scale * factor(1)

time: 102 us -> 101 us (level)
  Pallas kernels: 97.4 us -> 95.6 us
    pallas_call x1, Pallas kernels: 97.4 us -> 95.6 us  [local(): pl.pallas_call(functools.partial(kernel, n, rows, width, k, tuple(stages)...]
where the time goes in v2:
time: 101 us; the launch traced here: 100 us
  Pallas kernels  95.6 us (95%)
  local copies, waits for them, and re-layouts  4.77 us (5%)
    pallas_call x1, Pallas kernels, local(): pl.pallas_call(functools.partial(kernel, n, rows, width, k, tuple(stages)...  95.6 us
    unnamed x5, local copies, waits for them, and re-layouts  4.77 us

profile of v2, /device:TPU:0, one launch (start us, length us, event | category | flops | bytes accessed | tf_op | source)
XLA Modules:
  0.0 100.4 jit_solution(16445813338901706208)
XLA Ops:
  0.0 0.0 copy-start
  0.0 0.7 copy-done
  0.7 0.7 copy.6.pairs
  1.4 1.7 %copy.5 = bf16[1,1024,64]{2,1,0:T(8,128)(2,1)} copy(bf16[1,1024,64]{1,2,0:T(8,128)(2,1)} %param.6) | data formatting | bytes 262144 | tf_op args[2]
  3.1 95.6 %shard_map.46 = f32[64,1024]{1,0:T(8,128)} custom-call(s32[32,2]{1,0:T(8,128)} %copy.6.pairs, bf16[1,1024]{1,0:T(2,128)(2,1)} %scales.1, bf16[1024,64]{1,0:T(8,128)(2,1)} %bitcast.6, bf16[1024,384]{1,0:T(8,128)(2,1)} %bitcast.7), custom_call_target="tpu_custom_call" | custom-call | tf_op jit(solution)/shard_map/pallas_call | solution.py:388
  98.7 1.7 %copy.8 = f32[1,1024,64]{1,2,0:T(8,128)} copy(f32[1,1024,64]{1,2,0:T(8,128)} %bitcast.5) | data formatting | bytes 524288
Async XLA Ops:
  0.0 0.7 copy-start
